TPU v7x, 32 devices: a whole 2x2x4 slice. The times are simulated.
32 devices in a mesh: occ: 8 (over z, y), off: 4 (over x, core).
Axes of the slice: x: 2, y: 2, z: 4, core: 2. Of those that a mesh axis runs over, the one named last changes fastest.
Arguments:
- factors: bfloat16 [8, 768, 2048], P('occ'), may hold values from -0.8984375 to 0.8984375
- occ_level: int32 [8], replicated, may hold values from 0 to 255
- vir_level: int32 [768], replicated, may hold values from 0 to 255
- occupied_energy_levels: float32 [256], replicated, may hold values from -2 to -0.5
- vir_table: float32 [256], replicated, may hold values from 0.5 to 4
- virtual_coefficient_matrix: bfloat16 [768, 1024], replicated, may hold values from -0.21875 to 0.21875
Outputs:
- density_ao: float32 [8, 2048, 1024], P(None, ('occ', 'off'))
Inputs may be any that keep to these rules, and one draw needn't show every extreme that they name: `occ_level`: indices into occupied_energy_levels. `vir_level`: indices into vir_table.
All inputs are finite; a program needn't handle non-finite values.
Results may differ from a plain program's by a relative error of at most 0.0032.
Values may be sent and summed in bfloat16 or wider, within the bound.
A program may use at most 64 MiB of HBM per device.

v0:
```python
import jax
import jax.numpy as jnp
from jax import lax
from jax.sharding import PartitionSpec as P

PAIR_STEPS = 2


def passed_along(value, axis, by):
    length = lax.axis_size(axis)
    return lax.ppermute(value, axis, [(i, (i + by) % length) for i in range(length)])


def lookup(level, table):
    hits = level[:, None] == jnp.arange(table.shape[0], dtype=jnp.int32)[None, :]
    return jnp.sum(jnp.where(hits, table[None, :], jnp.float32(0.0)), axis=1)


def body(
    factors, occ_level, vir_level, occupied_energy_levels, vir_table, virtual_coefficient_matrix
):
    off_count = lax.axis_size("off")
    off_index = lax.axis_index("off")
    occ_count = lax.axis_size("occ")
    occ_index = lax.axis_index("occ")
    vir_energy = lookup(vir_level, vir_table)
    occ_energy = lookup(occ_level, occupied_energy_levels)
    own_energy = lax.dynamic_index_in_dim(occ_energy, occ_index, 0, keepdims=False)
    own = factors[0]
    carried = factors
    for bit_pos in range(off_count.bit_length() - 1):
        moved = passed_along(carried, "occ", 1 << bit_pos)
        carried = jnp.where(off_index >> bit_pos & 1 == 1, moved, carried)
    gamma = jnp.zeros((own.shape[1], own.shape[0]), jnp.float32)
    for step_index in range(PAIR_STEPS):
        offset = off_index + off_count * step_index
        pair_companion = (occ_index - offset) % occ_count
        other_energy = lax.dynamic_index_in_dim(occ_energy, pair_companion, 0, keepdims=False)
        other = carried[0]
        if step_index < PAIR_STEPS - 1:
            carried = passed_along(carried, "occ", off_count)
        integral = lax.dot_general(
            own, other, (((1,), (1,)), ((), ())), preferred_element_type=jnp.float32
        )
        denom = vir_energy[:, None] + vir_energy[None, :] - own_energy - other_energy
        amp = integral / denom
        pair_weight = (2.0 * amp - amp.T).astype(jnp.bfloat16)
        gamma = gamma + lax.dot_general(
            other, pair_weight, (((0,), (1,)), ((), ())), preferred_element_type=jnp.float32
        )
    naux_rows = gamma.shape[0]
    per_device = naux_rows // (occ_count * off_count)
    blocks = gamma.reshape(occ_count, off_count, per_device, gamma.shape[1])
    total = lax.psum(blocks, "off")
    mine = lax.dynamic_slice_in_dim(total, off_index, 1, 1)
    lower_gamma_part = mine.reshape(occ_count, per_device, gamma.shape[1]).astype(jnp.bfloat16)
    finished_flag = jnp.einsum(
        "sbd,dw->sbw",
        lower_gamma_part,
        virtual_coefficient_matrix,
        preferred_element_type=jnp.float32,
    )
    moved_back = lax.all_to_all(finished_flag[None], "occ", split_axis=1, concat_axis=0, tiled=True)
    return moved_back.reshape(moved_back.shape[0], per_device, virtual_coefficient_matrix.shape[1])


def solution(mesh):
    in_specs = (P("occ", None, None), P(), P(), P(), P(), P())
    out_specs = P(None, ("occ", "off"), None)
    return jax.shard_map(body, mesh=mesh, in_specs=in_specs, out_specs=out_specs, check_vma=False)
```

profile of v0, /device:TPU:0, one launch (start us, length us, event | category | flops | bytes accessed | tf_op | source)
XLA Modules:
  0.0 484.2 jit_solution(13570705393333818910)
XLA Ops:
  0.0 0.0 copy-start
  0.0 3.0 collective-permute-start
  3.0 71.5 %collective-permute-done = bf16[1,768,2048]{2,1,0:T(8,128)(2,1)} collective-permute-done((bf16[1,768,2048]{2,1,0:T(8,128)(2,1)}, bf16[1,768,2048]{2,1,0:T(8,128)(2,1)}, u32[]{:S(2)}, u32[]{:S(2)}) %collective-permute-start) | collective-permute-done | bytes 3145760 | tf_op jit(solution)/shard_map/ppermute | solution.py:11
  74.4 3.9 broadcast_select_fusion
  78.3 0.0 collective-permute-start.1
  78.3 0.0 copy-start.5
  78.3 0.0 copy-start.6
  78.3 0.0 copy-start.3
  78.3 0.0 copy-start.4
  78.4 71.4 %collective-permute-done.1 = bf16[1,768,2048]{2,1,0:T(8,128)(2,1)} collective-permute-done((bf16[1,768,2048]{2,1,0:T(8,128)(2,1)}, bf16[1,768,2048]{2,1,0:T(8,128)(2,1)}, u32[]{:S(2)}, u32[]{:S(2)}) %collective-permute-start.1) | collective-permute-done | bytes 3145760 | tf_op jit(solution)/shard_map/ppermute | solution.py:11
  149.7 3.9 broadcast_select_fusion.1
  153.6 0.0 collective-permute-start.2
  153.6 0.0 copy-done.5
  153.6 0.0 copy-done.6
  153.6 0.2 select_reduce_fusion.1
  153.8 0.7 fusion.33
  154.5 0.0 copy-done.3
  154.5 0.0 copy-done.4
  154.5 0.3 select_reduce_fusion
  154.8 6.9 %fusion.5 = f32[768,768]{1,0:T(8,128)} fusion(bf16[1,768,2048]{2,1,0:T(8,128)(2,1)} %param.6, bf16[1,768,2048]{2,1,0:T(8,128)(2,1)} %broadcast_select_fusion.1), kind=kOutput, calls=%fused_computation.6 | convolution fusion | flops 2415919104 | bytes 8650752 | tf_op jit(solution)/shard_map/dot_general | solution.py:42
  161.7 3.1 copy.14
  164.8 124.0 %collective-permute-done.2 = bf16[1,768,2048]{2,1,0:T(8,128)(2,1)} collective-permute-done((bf16[1,768,2048]{2,1,0:T(8,128)(2,1)}, bf16[1,768,2048]{2,1,0:T(8,128)(2,1)}, u32[]{:S(2)}, u32[]{:S(2)}) %collective-permute-start.2) | collective-permute-done | bytes 3145760 | tf_op jit(solution)/shard_map/ppermute | solution.py:11
  288.8 7.0 %fusion.2 = f32[768,768]{1,0:T(8,128)} fusion(bf16[1,768,2048]{2,1,0:T(8,128)(2,1)} %collective-permute-done.2, bf16[1,768,2048]{2,1,0:T(8,128)(2,1)} %param.6), kind=kOutput, calls=%fused_computation.3 | convolution fusion | flops 2415919104 | bytes 8650752 | tf_op jit(solution)/shard_map/dot_general | solution.py:42
  295.8 3.1 copy.15
  298.9 0.0 copy-start.1
  298.9 0.0 copy-start.2
  298.9 8.4 %fusion = f32[2048,768]{1,0:T(8,128)S(1)} fusion(bf16[1,768,2048]{2,1,0:T(8,128)(2,1)} %collective-permute-done.2, f32[768,768]{0,1:T(8,128)} %copy.15, f32[768,768]{1,0:T(8,128)} %fusion.2, f32[]{:T(128)} %bitcast.7, f32[]{:T(128)} %bitcast.3, f32[768]{0:T(1024)S(1)} %select_reduce_fusion), kind=kOutput, calls=%fused_computation.1 | convolution fusion | flops 2420637696 | bytes 14158856 | tf_op jit(solution)/shard_map/dot_general | solution.py:48
  307.3 0.0 copy-done.1
  307.3 0.0 copy-done.2
  307.3 6.7 %convolution_add_fusion = f32[2048,768]{1,0:T(8,128)S(1)} fusion(f32[2048,768]{1,0:T(8,128)S(1)} %fusion, bf16[1,768,2048]{2,1,0:T(8,128)(2,1)} %broadcast_select_fusion.1, f32[768,768]{0,1:T(8,128)S(1)} %copy-done.2, f32[768,768]{1,0:T(8,128)S(1)} %copy-done.1, f32[]{:T(128)} %bitcast.4, f32[]{:T(128)} %bitcast.3, f32[768]{0:T(1024)S(1)} %select_reduce_fusion), kind=kOutput, calls=%fused_computation | convolution fusion | flops 2422210560 | bytes 20450312 | tf_op jit(solution)/shard_map/dot_general | solution.py:48
  313.9 3.3 copy.16
  317.3 112.1 %all-reduce.1 = bf16[8,4,64,768]{3,2,0,1:T(8,128)(2,1)} all-reduce(f32[8,4,64,768]{3,2,0,1:T(8,128)} %copy.16), channel_id=1, replica_groups=mesh['occ'=8,'off'=4] {'off'}, use_global_device_ids=true, to_apply=%region_2.3 | all-reduce | flops 1572864 | bytes 9437184 | tf_op jit(solution)/shard_map/psum | solution.py:54
  429.3 0.0 copy-done
  429.3 2.1 convolution_bitcast_fusion
  431.4 51.5 %all_to_all.4 = f32[1,8,64,1024]{3,2,0,1:T(8,128)S(1)} all-to-all(f32[1,8,64,1024]{3,2,0,1:T(8,128)S(1)} %convolution_bitcast_fusion), channel_id=1, replica_groups=mesh['occ'=8,'off'=4] {'occ'}, dimensions={1} | all-to-all | bytes 4194304 | tf_op jit(solution)/shard_map/all_to_all | solution.py:63
  482.9 1.3 copy.21
Async XLA Ops:
  0.0 429.3 %copy-start = (bf16[768,1024]{1,0:T(8,128)(2,1)S(1)}, bf16[768,1024]{1,0:T(8,128)(2,1)}, u32[]{:S(2)}) copy-start(bf16[768,1024]{1,0:T(8,128)(2,1)} %param.11) | copy-start | bytes 4718596
  0.0 74.4 %collective-permute-start = (bf16[1,768,2048]{2,1,0:T(8,128)(2,1)}, bf16[1,768,2048]{2,1,0:T(8,128)(2,1)}, u32[]{:S(2)}, u32[]{:S(2)}) collective-permute-start(bf16[1,768,2048]{2,1,0:T(8,128)(2,1)} %param.6), channel_id=1, source_target_pairs={{0,4},{4,8},{8,12},{12,16},{16,20},{20,24},{24,28},{28,0},{1,5},{5... | collective-permute-start | bytes 9437192 | tf_op jit(solution)/shard_map/ppermute | solution.py:11
  78.3 71.4 %collective-permute-start.1 = (bf16[1,768,2048]{2,1,0:T(8,128)(2,1)}, bf16[1,768,2048]{2,1,0:T(8,128)(2,1)}, u32[]{:S(2)}, u32[]{:S(2)}) collective-permute-start(bf16[1,768,2048]{2,1,0:T(8,128)(2,1)} %broadcast_select_fusion), channel_id=1, source_target_pairs={{0,8},{4,12},{8,16},{12,20},{16,24},{20,28},{24,0},{28,4},{1,9},{5... | collective-permute-start | bytes 9437192 | tf_op jit(solution)/shard_map/ppermute | solution.py:11
  78.3 75.3 %copy-start.5 = (f32[256]{0:T(256)S(1)}, f32[256]{0:T(256)}, u32[]{:S(2)}) copy-start(f32[256]{0:T(256)} %param.9) | copy-start | bytes 3076
  78.3 75.3 %copy-start.6 = (s32[8]{0:T(128)S(1)}, s32[8]{0:T(128)}, u32[]{:S(2)}) copy-start(s32[8]{0:T(128)} %param.7) | copy-start | bytes 100
  78.3 76.2 %copy-start.3 = (s32[768]{0:T(1024)S(1)}, s32[768]{0:T(1024)}, u32[]{:S(2)}) copy-start(s32[768]{0:T(1024)} %param.8) | copy-start | bytes 9220
  78.3 76.1 %copy-start.4 = (f32[256]{0:T(256)S(1)}, f32[256]{0:T(256)}, u32[]{:S(2)}) copy-start(f32[256]{0:T(256)} %param.10) | copy-start | bytes 3076
  153.6 135.2 %collective-permute-start.2 = (bf16[1,768,2048]{2,1,0:T(8,128)(2,1)}, bf16[1,768,2048]{2,1,0:T(8,128)(2,1)}, u32[]{:S(2)}, u32[]{:S(2)}) collective-permute-start(bf16[1,768,2048]{2,1,0:T(8,128)(2,1)} %broadcast_select_fusion.1), channel_id=1, source_target_pairs={{0,16},{4,20},{8,24},{12,28},{16,0},{20,4},{24,8},{28,12},{1,17},{... | collective-permute-start | bytes 9437192 | tf_op jit(solution)/shard_map/ppermute | solution.py:11
  298.9 8.4 %copy-start.1 = (f32[768,768]{1,0:T(8,128)S(1)}, f32[768,768]{1,0:T(8,128)}, u32[]{:S(2)}) copy-start(f32[768,768]{1,0:T(8,128)} %fusion.5) | copy-start | bytes 7077892
  298.9 8.4 %copy-start.2 = (f32[768,768]{0,1:T(8,128)S(1)}, f32[768,768]{0,1:T(8,128)}, u32[]{:S(2)}) copy-start(f32[768,768]{0,1:T(8,128)} %copy.14) | copy-start | bytes 7077892
where the time goes:
time: 485 us; the launch traced here: 484 us
  waiting for transfers between devices  267 us (55%)
  blocking collectives  164 us (34%)
  matrix products  31 us (6%)
  local copies, waits for them, and re-layouts  11.5 us (2%)
  other arithmetic  8.27 us (2%)
    ppermute x3, waiting for transfers between devices, passed_along(): lax.ppermute(value, axis, [(i, (i + by) % length) for i in range(length)])  267 us
    psum x1, blocking collectives, body(): total = lax.psum(blocks, 'off')  112 us
    all_to_all x1, blocking collectives, body(): lax.all_to_all(finished_flag[None], 'occ', split_axis=1, concat_axis=0, t...  51.5 us
    dot_general x2, matrix products, body(): lax.dot_general(other, pair_weight, (((0,), (1,)), ((), ())), preferred_e...  15 us
    dot_general x2, matrix products, body(): lax.dot_general(own, other, (((1,), (1,)), ((), ())), preferred_element_t...  13.9 us
  transfers between devices with their start and end apart: 3, of which 3 were waited for; matrix products, arithmetic and copies ran while one was open for 2% of the time, Pallas kernels for 0%

commit v1 on v0

--- a/solution.py
+++ b/solution.py
@@ -1,9 +1,15 @@
+import functools
+
 import jax
 import jax.numpy as jnp
 from jax import lax
+from jax.experimental import pallas as pl
+from jax.experimental.pallas import tpu as pltpu
 from jax.sharding import PartitionSpec as P
 
 PAIR_STEPS = 2
+PIECES = 4
+MESH = pl.DeviceIdType.MESH
 
 
 def passed_along(value, axis, by):
@@ -16,7 +22,375 @@
     return jnp.sum(jnp.where(hits, table[None, :], jnp.float32(0.0)), axis=1)
 
 
-def body(
+def ring_place(occ, n):
+    return jnp.where(occ % 2 == 0, occ // 2, n - 1 - occ // 2)
+
+
+def ring_member(place, n):
+    return jnp.where(place < n // 2, 2 * place, 2 * (n - 1 - place) + 1)
+
+
+def pair_kernel(
+    n,
+    energy_ref,
+    factors_ref,
+    ev_row_ref,
+    ev_col_ref,
+    out_ref,
+    hold,
+    amp,
+    weight,
+    acc,
+    core_out,
+    core_in,
+    side_out,
+    side_in,
+    final,
+    land,
+    load_sem,
+    ring_send,
+    ring_recv,
+    side_send,
+    side_recv,
+    last_send,
+    last_recv,
+    core_sems,
+    cross_sems,
+    spread_send,
+    spread_recv,
+):
+    hops = n // 2
+    virt, naux = hold.shape[1], hold.shape[2]
+    half = virt // 2
+    piece = half // PIECES
+    share = PIECES // 2
+    rows = land.shape[1]
+    me = lax.axis_index("occ")
+    off = lax.axis_index("off")
+    side, core = off // 2, off % 2
+    place = ring_place(me, n)
+    up = ring_member(lax.rem(place + 1, n), n)
+    down = ring_member(lax.rem(place + n - 1, n), n)
+    onward = jnp.where(core == 0, up, down)
+    other_side = (1 - side) * 2 + core
+    other_core = side * 2 + (1 - core)
+
+    load = pltpu.make_async_copy(factors_ref.at[0], hold.at[0], load_sem)
+    load.start()
+
+    barrier = pltpu.get_barrier_semaphore()
+    for step in range(1, n):
+        pl.semaphore_signal(
+            barrier, inc=1, device_id=(lax.rem(me + step, n), off), device_id_type=MESH
+        )
+    for step in range(1, 4):
+        peer = lax.rem(off + step, 4)
+        for node in (me, up, down):
+            pl.semaphore_signal(barrier, inc=1, device_id=(node, peer), device_id_type=MESH)
+    pl.semaphore_wait(barrier, n - 1 + 9)
+    load.wait()
+
+    def ring_copy(slot, m):
+        where = pl.ds(pl.multiple_of(side * half + m * piece, piece), piece)
+        return pltpu.make_async_remote_copy(
+            src_ref=hold.at[slot, where],
+            dst_ref=hold.at[slot + 1, where],
+            send_sem=ring_send.at[slot, m],
+            recv_sem=ring_recv.at[slot, m],
+            device_id=(onward, off),
+            device_id_type=MESH,
+        )
+
+    def side_copy(slot, m, from_side):
+        where = pl.ds(pl.multiple_of(from_side * half + m * piece, piece), piece)
+        return pltpu.make_async_remote_copy(
+            src_ref=hold.at[slot, where],
+            dst_ref=hold.at[slot, where],
+            send_sem=side_send.at[slot - 1, m],
+            recv_sem=side_recv.at[slot - 1, m],
+            device_id=(me, other_side),
+            device_id_type=MESH,
+        )
+
+    def last_copy(t, from_side, from_core):
+        m = from_core * share + t
+        where = pl.ds(pl.multiple_of(from_side * half + m * piece, piece), piece)
+        return pltpu.make_async_remote_copy(
+            src_ref=hold.at[hops - 1, where],
+            dst_ref=hold.at[hops, where],
+            send_sem=last_send.at[t],
+            recv_sem=last_recv.at[from_side * PIECES + m],
+            device_id=(onward, 1),
+            device_id_type=MESH,
+        )
+
+    def handled(slot):
+        turn = lax.rem(slot + side + core, 2) == 1
+        inner = jnp.where(core == 0, slot < hops, slot > 0)
+        return jnp.logical_and(turn, inner)
+
+    def contribute(slot):
+        pair_energy = energy_ref[slot]
+
+        def integrals(h, _):
+            at = pl.ds(pl.multiple_of(h * half, half), half)
+            integral = lax.dot_general(
+                hold[slot, at, :],
+                hold[0],
+                (((1,), (1,)), ((), ())),
+                preferred_element_type=jnp.float32,
+            )
+            amp[at, :] = integral / (ev_col_ref[at, :] + ev_row_ref[...] - pair_energy)
+            return 0
+
+        lax.fori_loop(0, 2, integrals, 0)
+        third = virt // 3
+        for b in range(3):
+            for a in range(3):
+                bs, as_ = pl.ds(b * third, third), pl.ds(a * third, third)
+                weight[bs, as_] = (2.0 * amp[bs, as_] - amp[as_, bs].T).astype(jnp.bfloat16)
+
+        part = naux // 4
+
+        def gammas(p, _):
+            at = pl.ds(pl.multiple_of(p * part, part), part)
+            acc[at, :] += lax.dot_general(
+                hold[slot, :, at],
+                weight[...],
+                (((0,), (0,)), ((), ())),
+                preferred_element_type=jnp.float32,
+            )
+            return 0
+
+        lax.fori_loop(0, 4, gammas, 0)
+
+    for m in range(PIECES):
+        ring_copy(0, m).start()
+
+    def clear(p, _):
+        at = pl.ds(pl.multiple_of(p * 4 * rows, 4 * rows), 4 * rows)
+        acc[at, :] = jnp.zeros((4 * rows, virt), jnp.float32)
+        return 0
+
+    lax.fori_loop(0, n, clear, 0)
+
+    def stage(slot, _):
+        middle = jnp.logical_and(slot >= 1, slot < hops)
+
+        @pl.when(middle)
+        def _():
+            for m in range(PIECES):
+                ring_copy(slot - 1, m).wait_recv()
+
+                @pl.when(slot < hops - 1)
+                def _():
+                    ring_copy(slot, m).start()
+
+                @pl.when(jnp.logical_not(handled(slot)))
+                def _():
+                    side_copy(slot, m, side).start()
+
+        @pl.when(slot == hops - 1)
+        def _():
+            for t in range(share):
+                last_copy(t, side, core).start()
+
+        @pl.when(handled(slot))
+        def _():
+            @pl.when(middle)
+            def _():
+                for m in range(PIECES):
+                    side_copy(slot, m, 1 - side).wait_recv()
+
+            @pl.when(slot == hops)
+            def _():
+                for s in range(2):
+                    for c in range(2):
+                        for t in range(share):
+                            last_copy(t, s, c).wait_recv()
+
+            contribute(slot)
+
+        return 0
+
+    lax.fori_loop(0, hops + 1, stage, 0)
+
+    def core_copy(k):
+        return pltpu.make_async_remote_copy(
+            src_ref=core_out.at[k],
+            dst_ref=core_in.at[k],
+            send_sem=core_sems.at[0, k],
+            recv_sem=core_sems.at[1, k],
+            device_id=(me, other_core),
+            device_id_type=MESH,
+        )
+
+    def cross_copy(k):
+        return pltpu.make_async_remote_copy(
+            src_ref=side_out.at[k],
+            dst_ref=side_in.at[k],
+            send_sem=cross_sems.at[0, k],
+            recv_sem=cross_sems.at[1, k],
+            device_id=(me, other_side),
+            device_id_type=MESH,
+        )
+
+    def spread_copy(k, source):
+        return pltpu.make_async_remote_copy(
+            src_ref=final.at[k],
+            dst_ref=land.at[source],
+            send_sem=spread_send.at[k],
+            recv_sem=spread_recv.at[source],
+            device_id=(k, off),
+            device_id_type=MESH,
+        )
+
+    def chunk(k, s, c):
+        return pl.ds(pl.multiple_of(((k * 2 + s) * 2 + c) * rows, rows), rows)
+
+    def to_core(t, _):
+        k = lax.rem(me + 1 + t, n)
+        for s in range(2):
+            core_out[k, s] = acc[chunk(k, s, 1 - core), :].astype(jnp.bfloat16)
+        core_copy(k).start()
+        return 0
+
+    lax.fori_loop(0, n, to_core, 0)
+
+    def to_side(t, _):
+        k = lax.rem(me + 1 + t, n)
+        core_copy(k).wait_recv()
+        theirs = acc[chunk(k, 1 - side, core), :] + core_in[k, 1 - side].astype(jnp.float32)
+        side_out[k] = theirs.astype(jnp.bfloat16)
+        cross_copy(k).start()
+        return 0
+
+    lax.fori_loop(0, n, to_side, 0)
+
+    def to_owner(t, _):
+        k = lax.rem(me + 1 + t, n)
+        cross_copy(k).wait_recv()
+        mine = acc[chunk(k, side, core), :] + core_in[k, side].astype(jnp.float32)
+        mine = (mine + side_in[k].astype(jnp.float32)).astype(jnp.bfloat16)
+
+        @pl.when(t < n - 1)
+        def _():
+            final[k] = mine
+            spread_copy(k, me).start()
+
+        @pl.when(t == n - 1)
+        def _():
+            out_ref[me] = mine
+
+        return 0
+
+    lax.fori_loop(0, n, to_owner, 0)
+
+    def settle(t, _):
+        k = lax.rem(me + 1 + t, n)
+        spread_copy(k, k).wait_recv()
+        out_ref[k] = land[k]
+        return 0
+
+    lax.fori_loop(0, n - 1, settle, 0)
+
+    for slot in range(hops - 1):
+        for m in range(PIECES):
+            ring_copy(slot, m).wait_send()
+
+    def sent(slot, _):
+        @pl.when(jnp.logical_not(handled(slot)))
+        def _():
+            for m in range(PIECES):
+                side_copy(slot, m, side).wait_send()
+
+        return 0
+
+    lax.fori_loop(1, hops, sent, 0)
+    for t in range(share):
+        last_copy(t, side, core).wait_send()
+
+    def closed(t, _):
+        k = lax.rem(me + 1 + t, n)
+        core_copy(k).wait_send()
+        cross_copy(k).wait_send()
+
+        @pl.when(t < n - 1)
+        def _():
+            spread_copy(k, me).wait_send()
+
+        return 0
+
+    lax.fori_loop(0, n, closed, 0)
+
+
+def ring_body(
+    factors, occ_level, vir_level, occupied_energy_levels, vir_table, virtual_coefficient_matrix
+):
+    n = lax.axis_size("occ")
+    hops = n // 2
+    off = lax.axis_index("off")
+    me = lax.axis_index("occ")
+    virt, naux = factors.shape[1], factors.shape[2]
+    rows = naux // (n * lax.axis_size("off"))
+    ev = lookup(vir_level, vir_table)
+    eo = lookup(occ_level, occupied_energy_levels)
+    turn = jnp.where(off % 2 == 0, -1, 1)
+    partners = ring_member((ring_place(me, n) + turn * jnp.arange(hops + 1)) % n, n)
+    own_energy = lax.dynamic_index_in_dim(eo, me, 0, keepdims=False)
+    hit = partners[:, None] == jnp.arange(n)[None, :]
+    energy = own_energy + jnp.sum(jnp.where(hit, eo[None, :], jnp.float32(0.0)), axis=1)
+    vmem = pl.BlockSpec(memory_space=pltpu.VMEM)
+    dma = pltpu.SemaphoreType.DMA
+    gamma_low = pl.pallas_call(
+        functools.partial(pair_kernel, n),
+        out_shape=jax.ShapeDtypeStruct((n, rows, virt), jnp.bfloat16),
+        in_specs=[
+            pl.BlockSpec(memory_space=pltpu.SMEM),
+            pl.BlockSpec(memory_space=pl.ANY),
+            vmem,
+            vmem,
+        ],
+        out_specs=vmem,
+        scratch_shapes=[
+            pltpu.VMEM((hops + 1, virt, naux), jnp.bfloat16),
+            pltpu.VMEM((virt, virt), jnp.float32),
+            pltpu.VMEM((virt, virt), jnp.bfloat16),
+            pltpu.VMEM((naux, virt), jnp.float32),
+            pltpu.VMEM((n, 2, rows, virt), jnp.bfloat16),
+            pltpu.VMEM((n, 2, rows, virt), jnp.bfloat16),
+            pltpu.VMEM((n, rows, virt), jnp.bfloat16),
+            pltpu.VMEM((n, rows, virt), jnp.bfloat16),
+            pltpu.VMEM((n, rows, virt), jnp.bfloat16),
+            pltpu.VMEM((n, rows, virt), jnp.bfloat16),
+            dma,
+            dma((hops - 1, PIECES)),
+            dma((hops - 1, PIECES)),
+            dma((hops - 1, PIECES)),
+            dma((hops - 1, PIECES)),
+            dma((PIECES // 2,)),
+            dma((2 * PIECES,)),
+            dma((2, n)),
+            dma((2, n)),
+            dma((n,)),
+            dma((n,)),
+        ],
+        compiler_params=pltpu.CompilerParams(
+            collective_id=0, has_side_effects=True, vmem_limit_bytes=56 * 1024 * 1024
+        ),
+        cost_estimate=pl.CostEstimate(
+            flops=8 * virt * virt * naux, bytes_accessed=2 * virt * naux, transcendentals=0
+        ),
+    )(energy, factors, ev[None, :], ev[:, None])
+    return jnp.einsum(
+        "sbd,dw->sbw",
+        gamma_low,
+        virtual_coefficient_matrix,
+        preferred_element_type=jnp.float32,
+    )
+
+
+def general_body(
     factors, occ_level, vir_level, occupied_energy_levels, vir_table, virtual_coefficient_matrix
 ):
     off_count = lax.axis_size("off")
@@ -67,4 +441,7 @@
 def solution(mesh):
     in_specs = (P("occ", None, None), P(), P(), P(), P(), P())
     out_specs = P(None, ("occ", "off"), None)
+    every_pair = mesh.shape["occ"] == mesh.shape["off"] * PAIR_STEPS
+    ring = every_pair and mesh.shape["off"] == 4
+    body = ring_body if ring else general_body
     return jax.shard_map(body, mesh=mesh, in_specs=in_specs, out_specs=out_specs, check_vma=False)

time: 485 us -> 152 us (0.31)
  waiting for transfers between devices: 267 us -> 0 us
  blocking collectives: 164 us -> 0 us
  Pallas kernels: 0 us -> 141 us
  matrix products: 31 us -> 3.44 us
  local copies, waits for them, and re-layouts: 11.5 us -> 2.1 us
  other arithmetic: 8.27 us -> 3.3 us
    ppermute x3 -> x0, waiting for transfers between devices: 267 us -> none  [passed_along(): lax.ppermute(value, axis, [(i, (i + by) % length) for i in range(length)])]
    pallas_call x0 -> x1, Pallas kernels: none -> 141 us  [ring_body(): pl.pallas_call(functools.partial(pair_kernel, n), out_shape=jax.ShapeDtyp...]
    psum x1 -> x0, blocking collectives: 112 us -> none  [body(): total = lax.psum(blocks, 'off')]
    all_to_all x1 -> x0, blocking collectives: 51.5 us -> none  [body(): lax.all_to_all(finished_flag[None], 'occ', split_axis=1, concat_axis=0, t...]
    dot_general x5 -> x1, matrix products: 31 us -> 3.44 us  [ring_body(): jnp.einsum('sbd,dw->sbw', gamma_low, virtual_coefficient_matrix, preferre...]
    select_n x2 -> x1, other arithmetic: 7.79 us -> 0.01 us  [ring_member(): return jnp.where(place < n // 2, 2 * place, 2 * (n - 1 - place) + 1)]
    dot_general x2 -> x0, local copies, waits for them, and re-layouts: 6.19 us -> none  [body(): lax.dot_general(own, other, (((1,), (1,)), ((), ())), preferred_element_t...]
  transfers between devices with their start and end apart: 3 -> 0, of which waited for: 3 -> 0; matrix products, arithmetic and copies ran while one was open for 2% -> 0% of each run, Pallas kernels for 0% -> 0%
where the time goes in v1:
time: 152 us; the launch traced here: 150 us
  Pallas kernels  141 us (93%)
  matrix products  3.44 us (2%)
  other arithmetic  3.3 us (2%)
  local copies, waits for them, and re-layouts  2.1 us (1%)
    pallas_call x1, Pallas kernels, ring_body(): pl.pallas_call(functools.partial(pair_kernel, n), out_shape=jax.ShapeDtyp...  141 us
    dot_general x1, matrix products, ring_body(): jnp.einsum('sbd,dw->sbw', gamma_low, virtual_coefficient_matrix, preferre...  3.44 us

profile of v1, /device:TPU:0, one launch (start us, length us, event | category | flops | bytes accessed | tf_op | source)
XLA Modules:
  0.0 150.1 jit_solution(5777231641920769804)
XLA Ops:
  0.0 0.0 copy-start
  0.0 1.0 select_reduce_fusion.1
  1.0 0.6 dynamic_slice.4
  1.6 0.2 select_reduce_fusion.2
  1.8 1.1 broadcast_add_fusion.energy_ref
  2.9 1.0 select_reduce_fusion
  3.9 0.6 broadcast_in_dim.57.ev_row_ref
  4.5 0.9 broadcast_in_dim.59.ev_col_ref
  5.4 141.2 %shard_map.64 = bf16[8,64,768]{2,1,0:T(8,128)(2,1)} custom-call(f32[5]{0:T(128)} %broadcast_add_fusion.energy_ref, bf16[1,768,2048]{2,1,0:T(8,128)(2,1)} %factors_ref.1, f32[1,768]{1,0:T(1,128)} %broadcast_in_dim.57.ev_row_ref, f32[768,1]{1,0:T(8,128)} %broadcast_in_dim.59.ev_col_ref), custom_call_target="tpu_custom_call" | custom-call | flops 9663676416 | bytes 3145728 | tf_op jit(solution)/shard_map/pallas_call | solution.py:345
  146.6 0.0 copy-done
  146.6 3.4 %fusion = f32[8,64,1024]{2,1,0:T(8,128)} fusion(bf16[8,64,768]{2,1,0:T(8,128)(2,1)} %shard_map.64, bf16[768,1024]{1,0:T(8,128)(2,1)S(1)} %copy-done), kind=kOutput, calls=%fused_computation | convolution fusion | flops 805306368 | bytes 4456448 | tf_op jit(solution)/shard_map/sbd,dw->sbw/dot_general | solution.py:385
  (1 shorter events, 0.0 us)
Async XLA Ops:
  0.0 146.6 %copy-start = (bf16[768,1024]{1,0:T(8,128)(2,1)S(1)}, bf16[768,1024]{1,0:T(8,128)(2,1)}, u32[]{:S(2)}) copy-start(bf16[768,1024]{1,0:T(8,128)(2,1)} %param.11) | copy-start | bytes 4718596

commit v2 on v1

--- a/solution.py
+++ b/solution.py
@@ -32,11 +32,14 @@
 
 def pair_kernel(
     n,
-    energy_ref,
+    occ_level_ref,
+    occ_table_ref,
     factors_ref,
+    vir_level_ref,
+    vir_table_ref,
+    out_ref,
     ev_row_ref,
     ev_col_ref,
-    out_ref,
     hold,
     amp,
     weight,
@@ -54,6 +57,7 @@
     side_recv,
     last_send,
     last_recv,
+    pass_send,
     core_sems,
     cross_sems,
     spread_send,
@@ -120,7 +124,19 @@
             dst_ref=hold.at[hops, where],
             send_sem=last_send.at[t],
             recv_sem=last_recv.at[from_side * PIECES + m],
-            device_id=(onward, 1),
+            device_id=(onward, jnp.where(side == 0, 1, off)),
+            device_id_type=MESH,
+        )
+
+    def pass_copy(t):
+        m = core * share + t
+        where = pl.ds(pl.multiple_of(side * half + m * piece, piece), piece)
+        return pltpu.make_async_remote_copy(
+            src_ref=hold.at[hops, where],
+            dst_ref=hold.at[hops, where],
+            send_sem=pass_send.at[t],
+            recv_sem=last_recv.at[side * PIECES + m],
+            device_id=(me, 1),
             device_id_type=MESH,
         )
 
@@ -129,40 +145,58 @@
         inner = jnp.where(core == 0, slot < hops, slot > 0)
         return jnp.logical_and(turn, inner)
 
-    def contribute(slot):
-        pair_energy = energy_ref[slot]
-
-        def integrals(h, _):
-            at = pl.ds(pl.multiple_of(h * half, half), half)
-            integral = lax.dot_general(
-                hold[slot, at, :],
-                hold[0],
-                (((1,), (1,)), ((), ())),
-                preferred_element_type=jnp.float32,
-            )
-            amp[at, :] = integral / (ev_col_ref[at, :] + ev_row_ref[...] - pair_energy)
-            return 0
-
-        lax.fori_loop(0, 2, integrals, 0)
+    def occ_energy(orbital):
+        return occ_table_ref[occ_level_ref[orbital]]
+
+    def integrals(slot, h):
+        turn = jnp.where(core == 0, n - slot, slot)
+        partner = ring_member(lax.rem(place + turn, n), n)
+        pair_energy = occ_energy(me) + occ_energy(partner)
+        at = pl.ds(pl.multiple_of(h * half, half), half)
+        integral = lax.dot_general(
+            hold[slot, at, :],
+            hold[0],
+            (((1,), (1,)), ((), ())),
+            preferred_element_type=jnp.float32,
+        )
+        amp[at, :] = integral / (ev_col_ref[at, :] + ev_row_ref[...] - pair_energy)
+
+    def weights():
         third = virt // 3
         for b in range(3):
             for a in range(3):
                 bs, as_ = pl.ds(b * third, third), pl.ds(a * third, third)
                 weight[bs, as_] = (2.0 * amp[bs, as_] - amp[as_, bs].T).astype(jnp.bfloat16)
 
-        part = naux // 4
-
-        def gammas(p, _):
-            at = pl.ds(pl.multiple_of(p * part, part), part)
-            acc[at, :] += lax.dot_general(
-                hold[slot, :, at],
-                weight[...],
-                (((0,), (0,)), ((), ())),
-                preferred_element_type=jnp.float32,
-            )
-            return 0
-
-        lax.fori_loop(0, 4, gammas, 0)
+    def gammas(slot, p, part):
+        at = pl.ds(pl.multiple_of(p * part, part), part)
+        acc[at, :] += lax.dot_general(
+            hold[slot, :, at],
+            weight[...],
+            (((0,), (0,)), ((), ())),
+            preferred_element_type=jnp.float32,
+        )
+
+    def work(slot, m):
+        if m == 0:
+            integrals(slot, side)
+        elif m == 1:
+
+            @pl.when(slot > 0)
+            def _():
+                for q in range(PIECES):
+                    side_copy(slot, q, 1 - side).wait_recv()
+
+            integrals(slot, 1 - side)
+        else:
+            if m == 2:
+                weights()
+
+            def two(p, _):
+                gammas(slot, 2 * (m - 2) + p, naux // 4)
+                return 0
+
+            lax.fori_loop(0, 2, two, 0)
 
     for m in range(PIECES):
         ring_copy(0, m).start()
@@ -174,12 +208,24 @@
 
     lax.fori_loop(0, n, clear, 0)
 
+    levels = vir_table_ref.shape[1]
+    same = lax.broadcasted_iota(jnp.int32, (levels, levels), 0) == lax.broadcasted_iota(
+        jnp.int32, (levels, levels), 1
+    )
+    table = jnp.sum(jnp.where(same, vir_table_ref[...], 0.0), axis=1, keepdims=True)
+    hits = lax.broadcasted_iota(jnp.int32, (levels, virt), 0) == vir_level_ref[...]
+    row = jnp.sum(jnp.where(hits, table, 0.0), axis=0, keepdims=True)
+    ev_row_ref[...] = row
+    same = lax.broadcasted_iota(jnp.int32, (virt, virt), 0) == lax.broadcasted_iota(
+        jnp.int32, (virt, virt), 1
+    )
+    ev_col_ref[...] = jnp.sum(jnp.where(same, row, 0.0), axis=1, keepdims=True)
+
     def stage(slot, _):
-        middle = jnp.logical_and(slot >= 1, slot < hops)
-
-        @pl.when(middle)
-        def _():
-            for m in range(PIECES):
+        for m in range(PIECES):
+
+            @pl.when(slot < hops)
+            def _():
                 ring_copy(slot - 1, m).wait_recv()
 
                 @pl.when(slot < hops - 1)
@@ -190,30 +236,38 @@
                 def _():
                     side_copy(slot, m, side).start()
 
-        @pl.when(slot == hops - 1)
-        def _():
-            for t in range(share):
-                last_copy(t, side, core).start()
-
-        @pl.when(handled(slot))
-        def _():
-            @pl.when(middle)
+            if m < share:
+
+                @pl.when(jnp.logical_and(slot == hops, side == 1))
+                def _():
+                    last_copy(m, side, core).wait_recv()
+                    pass_copy(m).start()
+
+            if m == PIECES - 1:
+
+                @pl.when(slot == hops - 1)
+                def _():
+                    for t in range(share):
+                        last_copy(t, side, core).start()
+
+            @pl.when(handled(slot - 1))
             def _():
-                for m in range(PIECES):
-                    side_copy(slot, m, 1 - side).wait_recv()
-
-            @pl.when(slot == hops)
-            def _():
-                for s in range(2):
-                    for c in range(2):
-                        for t in range(share):
-                            last_copy(t, s, c).wait_recv()
-
-            contribute(slot)
-
-        return 0
-
-    lax.fori_loop(0, hops + 1, stage, 0)
+                work(slot - 1, m)
+
+        return 0
+
+    lax.fori_loop(1, hops + 1, stage, 0)
+
+    late = handled(hops)
+
+    @pl.when(late)
+    def _():
+        for s in range(2):
+            for c in range(2):
+                for t in range(share):
+                    last_copy(t, s, c).wait_recv()
+            integrals(hops, s)
+        weights()
 
     def core_copy(k):
         return pltpu.make_async_remote_copy(
@@ -248,17 +302,23 @@
     def chunk(k, s, c):
         return pl.ds(pl.multiple_of(((k * 2 + s) * 2 + c) * rows, rows), rows)
 
-    def to_core(t, _):
-        k = lax.rem(me + 1 + t, n)
+    def target(t):
+        flip = jnp.where(t < n // 2, n // 2 + t, n - 1 - t)
+        k = 0
+        for bit in range(n.bit_length() - 1):
+            k = k + ((me // 2**bit + flip // 2**bit) % 2) * 2**bit
+        return k
+
+    def to_side(t, _):
+        k = target(t)
+
+        @pl.when(late)
+        def _():
+            gammas(hops, k, 4 * rows)
+
         for s in range(2):
             core_out[k, s] = acc[chunk(k, s, 1 - core), :].astype(jnp.bfloat16)
         core_copy(k).start()
-        return 0
-
-    lax.fori_loop(0, n, to_core, 0)
-
-    def to_side(t, _):
-        k = lax.rem(me + 1 + t, n)
         core_copy(k).wait_recv()
         theirs = acc[chunk(k, 1 - side, core), :] + core_in[k, 1 - side].astype(jnp.float32)
         side_out[k] = theirs.astype(jnp.bfloat16)
@@ -268,7 +328,7 @@
     lax.fori_loop(0, n, to_side, 0)
 
     def to_owner(t, _):
-        k = lax.rem(me + 1 + t, n)
+        k = target(t)
         cross_copy(k).wait_recv()
         mine = acc[chunk(k, side, core), :] + core_in[k, side].astype(jnp.float32)
         mine = (mine + side_in[k].astype(jnp.float32)).astype(jnp.bfloat16)
@@ -287,7 +347,7 @@
     lax.fori_loop(0, n, to_owner, 0)
 
     def settle(t, _):
-        k = lax.rem(me + 1 + t, n)
+        k = target(t)
         spread_copy(k, k).wait_recv()
         out_ref[k] = land[k]
         return 0
@@ -310,8 +370,13 @@
     for t in range(share):
         last_copy(t, side, core).wait_send()
 
+        @pl.when(side == 1)
+        def _():
+            pass_copy(t).wait_send()
+
+
     def closed(t, _):
-        k = lax.rem(me + 1 + t, n)
+        k = target(t)
         core_copy(k).wait_send()
         cross_copy(k).wait_send()
 
@@ -329,30 +394,25 @@
 ):
     n = lax.axis_size("occ")
     hops = n // 2
-    off = lax.axis_index("off")
-    me = lax.axis_index("occ")
     virt, naux = factors.shape[1], factors.shape[2]
     rows = naux // (n * lax.axis_size("off"))
-    ev = lookup(vir_level, vir_table)
-    eo = lookup(occ_level, occupied_energy_levels)
-    turn = jnp.where(off % 2 == 0, -1, 1)
-    partners = ring_member((ring_place(me, n) + turn * jnp.arange(hops + 1)) % n, n)
-    own_energy = lax.dynamic_index_in_dim(eo, me, 0, keepdims=False)
-    hit = partners[:, None] == jnp.arange(n)[None, :]
-    energy = own_energy + jnp.sum(jnp.where(hit, eo[None, :], jnp.float32(0.0)), axis=1)
+    smem = pl.BlockSpec(memory_space=pltpu.SMEM)
     vmem = pl.BlockSpec(memory_space=pltpu.VMEM)
     dma = pltpu.SemaphoreType.DMA
     gamma_low = pl.pallas_call(
         functools.partial(pair_kernel, n),
         out_shape=jax.ShapeDtypeStruct((n, rows, virt), jnp.bfloat16),
         in_specs=[
-            pl.BlockSpec(memory_space=pltpu.SMEM),
+            smem,
+            smem,
             pl.BlockSpec(memory_space=pl.ANY),
             vmem,
             vmem,
         ],
         out_specs=vmem,
         scratch_shapes=[
+            pltpu.VMEM((1, virt), jnp.float32),
+            pltpu.VMEM((virt, 1), jnp.float32),
             pltpu.VMEM((hops + 1, virt, naux), jnp.bfloat16),
             pltpu.VMEM((virt, virt), jnp.float32),
             pltpu.VMEM((virt, virt), jnp.bfloat16),
@@ -370,6 +430,7 @@
             dma((hops - 1, PIECES)),
             dma((PIECES // 2,)),
             dma((2 * PIECES,)),
+            dma((PIECES // 2,)),
             dma((2, n)),
             dma((2, n)),
             dma((n,)),
@@ -381,7 +442,7 @@
         cost_estimate=pl.CostEstimate(
             flops=8 * virt * virt * naux, bytes_accessed=2 * virt * naux, transcendentals=0
         ),
-    )(energy, factors, ev[None, :], ev[:, None])
+    )(occ_level, occupied_energy_levels, factors, vir_level[None, :], vir_table[None, :])
     return jnp.einsum(
         "sbd,dw->sbw",
         gamma_low,

time: 152 us -> 124 us (0.82)
  the two profiles are of different devices: /device:TPU:0 before, /device:TPU:13 now
where the time goes in v2:
time: 124 us
  Pallas kernels  119 us (96%)
  matrix products  3.44 us (3%)
  local copies, waits for them, and re-layouts  1.39 us (1%)
    pallas_call x1, Pallas kernels, ring_body(): pl.pallas_call(functools.partial(pair_kernel, n), out_shape=jax.ShapeDtyp...  119 us
    dot_general x1, matrix products, ring_body(): jnp.einsum('sbd,dw->sbw', gamma_low, virtual_coefficient_matrix, preferre...  3.44 us

profile of v2, /device:TPU:13, one launch (start us, length us, event | category | flops | bytes accessed | tf_op | source)
XLA Modules:
  0.0 124.2 jit_solution(8481974712523363283)
XLA Ops:
  0.0 0.0 copy-start
  0.0 1.4 %broadcast_in_dim.6.vir_level_ref = s32[1,768]{1,0:T(1,128)} reshape(s32[768]{0:T(1024)} %param.8) | data formatting | bytes 6144 | tf_op jit(solution)/shard_map/broadcast_in_dim | solution.py:445
  1.4 119.4 %shard_map.64 = bf16[8,64,768]{2,1,0:T(8,128)(2,1)} custom-call(s32[8]{0:T(128)} %occ_level_ref.1, f32[256]{0:T(256)} %occ_table_ref.1, bf16[1,768,2048]{2,1,0:T(8,128)(2,1)} %factors_ref.1, s32[1,768]{1,0:T(1,128)} %broadcast_in_dim.6.vir_level_ref, f32[1,256]{1,0:T(1,128)} %bitcast.5), custom_call_target="tpu_custom_call" | custom-call | flops 9663676416 | bytes 3145728 | tf_op jit(solution)/shard_map/pallas_call | solution.py:402
  120.8 0.0 copy-done
  120.8 3.4 %fusion = f32[8,64,1024]{2,1,0:T(8,128)} fusion(bf16[8,64,768]{2,1,0:T(8,128)(2,1)} %shard_map.64, bf16[768,1024]{1,0:T(8,128)(2,1)S(1)} %copy-done), kind=kOutput, calls=%fused_computation | convolution fusion | flops 805306368 | bytes 4456448 | tf_op jit(solution)/shard_map/sbd,dw->sbw/dot_general | solution.py:446
Async XLA Ops:
  0.0 120.8 %copy-start = (bf16[768,1024]{1,0:T(8,128)(2,1)S(1)}, bf16[768,1024]{1,0:T(8,128)(2,1)}, u32[]{:S(2)}) copy-start(bf16[768,1024]{1,0:T(8,128)(2,1)} %param.11) | copy-start | bytes 4718596

commit v3 on v2

--- a/solution.py
+++ b/solution.py
@@ -57,7 +57,6 @@
     side_recv,
     last_send,
     last_recv,
-    pass_send,
     core_sems,
     cross_sems,
     spread_send,
@@ -67,7 +66,6 @@
     virt, naux = hold.shape[1], hold.shape[2]
     half = virt // 2
     piece = half // PIECES
-    share = PIECES // 2
     rows = land.shape[1]
     me = lax.axis_index("occ")
     off = lax.axis_index("off")
@@ -116,34 +114,20 @@
             device_id_type=MESH,
         )
 
-    def last_copy(t, from_side, from_core):
-        m = from_core * share + t
-        where = pl.ds(pl.multiple_of(from_side * half + m * piece, piece), piece)
+    def last_copy(m, part):
+        where = pl.ds(pl.multiple_of(part * half + m * piece, piece), piece)
         return pltpu.make_async_remote_copy(
             src_ref=hold.at[hops - 1, where],
             dst_ref=hold.at[hops, where],
-            send_sem=last_send.at[t],
-            recv_sem=last_recv.at[from_side * PIECES + m],
-            device_id=(onward, jnp.where(side == 0, 1, off)),
-            device_id_type=MESH,
-        )
-
-    def pass_copy(t):
-        m = core * share + t
-        where = pl.ds(pl.multiple_of(side * half + m * piece, piece), piece)
-        return pltpu.make_async_remote_copy(
-            src_ref=hold.at[hops, where],
-            dst_ref=hold.at[hops, where],
-            send_sem=pass_send.at[t],
-            recv_sem=last_recv.at[side * PIECES + m],
-            device_id=(me, 1),
+            send_sem=last_send.at[m],
+            recv_sem=last_recv.at[part * PIECES + m],
+            device_id=(onward, side * 2 + (1 - side)),
             device_id_type=MESH,
         )
 
     def handled(slot):
         turn = lax.rem(slot + side + core, 2) == 1
-        inner = jnp.where(core == 0, slot < hops, slot > 0)
-        return jnp.logical_and(turn, inner)
+        return jnp.logical_and(turn, jnp.logical_or(core == 0, slot > 0))
 
     def occ_energy(orbital):
         return occ_table_ref[occ_level_ref[orbital]]
@@ -182,7 +166,7 @@
             integrals(slot, side)
         elif m == 1:
 
-            @pl.when(slot > 0)
+            @pl.when(jnp.logical_and(slot > 0, slot < hops - 1))
             def _():
                 for q in range(PIECES):
                     side_copy(slot, q, 1 - side).wait_recv()
@@ -236,19 +220,17 @@
                 def _():
                     side_copy(slot, m, side).start()
 
-            if m < share:
-
-                @pl.when(jnp.logical_and(slot == hops, side == 1))
+            @pl.when(jnp.logical_and(slot == hops - 1, jnp.logical_not(handled(slot))))
+            def _():
+                last_copy(m, 1 - core).start()
+
+            if m == 0:
+
+                @pl.when(jnp.logical_and(slot == hops, handled(hops - 1)))
                 def _():
-                    last_copy(m, side, core).wait_recv()
-                    pass_copy(m).start()
-
-            if m == PIECES - 1:
-
-                @pl.when(slot == hops - 1)
-                def _():
-                    for t in range(share):
-                        last_copy(t, side, core).start()
+                    for q in range(PIECES):
+                        side_copy(hops - 1, q, 1 - side).wait_recv()
+                        last_copy(q, 1 - core).start()
 
             @pl.when(handled(slot - 1))
             def _():
@@ -260,21 +242,12 @@
 
     late = handled(hops)
 
-    @pl.when(late)
-    def _():
-        for s in range(2):
-            for c in range(2):
-                for t in range(share):
-                    last_copy(t, s, c).wait_recv()
-            integrals(hops, s)
-        weights()
-
-    def core_copy(k):
+    def core_copy(k, s, when):
         return pltpu.make_async_remote_copy(
-            src_ref=core_out.at[k],
-            dst_ref=core_in.at[k],
-            send_sem=core_sems.at[0, k],
-            recv_sem=core_sems.at[1, k],
+            src_ref=core_out.at[k, s],
+            dst_ref=core_in.at[k, s],
+            send_sem=core_sems.at[2 * when, k],
+            recv_sem=core_sems.at[2 * when + 1, k],
             device_id=(me, other_core),
             device_id_type=MESH,
         )
@@ -309,17 +282,17 @@
             k = k + ((me // 2**bit + flip // 2**bit) % 2) * 2**bit
         return k
 
+    def to_core(t, _):
+        k = target(t)
+        core_out[k, 1 - side] = acc[chunk(k, 1 - side, 1 - core), :].astype(jnp.bfloat16)
+        core_copy(k, 1 - side, 0).start()
+        return 0
+
+    lax.fori_loop(0, n, to_core, 0)
+
     def to_side(t, _):
         k = target(t)
-
-        @pl.when(late)
-        def _():
-            gammas(hops, k, 4 * rows)
-
-        for s in range(2):
-            core_out[k, s] = acc[chunk(k, s, 1 - core), :].astype(jnp.bfloat16)
-        core_copy(k).start()
-        core_copy(k).wait_recv()
+        core_copy(k, 1 - side, 0).wait_recv()
         theirs = acc[chunk(k, 1 - side, core), :] + core_in[k, 1 - side].astype(jnp.float32)
         side_out[k] = theirs.astype(jnp.bfloat16)
         cross_copy(k).start()
@@ -327,9 +300,40 @@
 
     lax.fori_loop(0, n, to_side, 0)
 
+    @pl.when(late)
+    def _():
+        for part in range(2):
+            for m in range(PIECES):
+                last_copy(m, part).wait_recv()
+            integrals(hops, part)
+        weights()
+
+    def to_core_late(t, _):
+        @pl.when(late)
+        def _():
+            spots = []
+            for u in range(2):
+                base = target(2 * t + u) * 4 * rows + side * 2 * rows
+                spots.append(pl.ds(pl.multiple_of(base, 2 * rows), 2 * rows))
+            lanes = jnp.concatenate([hold[hops, :, spot] for spot in spots], axis=1)
+            more = lax.dot_general(
+                lanes, weight[...], (((0,), (0,)), ((), ())), preferred_element_type=jnp.float32
+            )
+            for u in range(2):
+                acc[spots[u], :] += more[u * 2 * rows : (u + 1) * 2 * rows, :]
+
+        for u in range(2):
+            k = target(2 * t + u)
+            core_out[k, side] = acc[chunk(k, side, 1 - core), :].astype(jnp.bfloat16)
+            core_copy(k, side, 1).start()
+        return 0
+
+    lax.fori_loop(0, n // 2, to_core_late, 0)
+
     def to_owner(t, _):
         k = target(t)
         cross_copy(k).wait_recv()
+        core_copy(k, side, 1).wait_recv()
         mine = acc[chunk(k, side, core), :] + core_in[k, side].astype(jnp.float32)
         mine = (mine + side_in[k].astype(jnp.float32)).astype(jnp.bfloat16)
 
@@ -367,17 +371,13 @@
         return 0
 
     lax.fori_loop(1, hops, sent, 0)
-    for t in range(share):
-        last_copy(t, side, core).wait_send()
-
-        @pl.when(side == 1)
-        def _():
-            pass_copy(t).wait_send()
-
+    for m in range(PIECES):
+        last_copy(m, 1 - core).wait_send()
 
     def closed(t, _):
         k = target(t)
-        core_copy(k).wait_send()
+        core_copy(k, 1 - side, 0).wait_send()
+        core_copy(k, side, 1).wait_send()
         cross_copy(k).wait_send()
 
         @pl.when(t < n - 1)
@@ -428,10 +428,9 @@
             dma((hops - 1, PIECES)),
             dma((hops - 1, PIECES)),
             dma((hops - 1, PIECES)),
-            dma((PIECES // 2,)),
+            dma((PIECES,)),
             dma((2 * PIECES,)),
-            dma((PIECES // 2,)),
-            dma((2, n)),
+            dma((4, n)),
             dma((2, n)),
             dma((n,)),
             dma((n,)),

time: 124 us -> 108 us (0.87)
  the two profiles are of different devices: /device:TPU:13 before, /device:TPU:0 now
where the time goes in v3:
time: 108 us
  Pallas kernels  103 us (95%)
  matrix products  3.44 us (3%)
  local copies, waits for them, and re-layouts  1.39 us (1%)
    pallas_call x1, Pallas kernels, ring_body(): pl.pallas_call(functools.partial(pair_kernel, n), out_shape=jax.ShapeDtyp...  103 us
    dot_general x1, matrix products, ring_body(): jnp.einsum('sbd,dw->sbw', gamma_low, virtual_coefficient_matrix, preferre...  3.44 us

profile of v3, /device:TPU:0, one launch (start us, length us, event | category | flops | bytes accessed | tf_op | source)
XLA Modules:
  0.0 108.0 jit_solution(8005912584942469718)
XLA Ops:
  0.0 0.0 copy-start
  0.0 1.4 %broadcast_in_dim.6.vir_level_ref = s32[1,768]{1,0:T(1,128)} reshape(s32[768]{0:T(1024)} %param.8) | data formatting | bytes 6144 | tf_op jit(solution)/shard_map/broadcast_in_dim | solution.py:444
  1.4 103.2 %shard_map.64 = bf16[8,64,768]{2,1,0:T(8,128)(2,1)} custom-call(s32[8]{0:T(128)} %occ_level_ref.1, f32[256]{0:T(256)} %occ_table_ref.1, bf16[1,768,2048]{2,1,0:T(8,128)(2,1)} %factors_ref.1, s32[1,768]{1,0:T(1,128)} %broadcast_in_dim.6.vir_level_ref, f32[1,256]{1,0:T(1,128)} %bitcast.5), custom_call_target="tpu_custom_call" | custom-call | flops 9663676416 | bytes 3145728 | tf_op jit(solution)/shard_map/pallas_call | solution.py:402
  104.6 0.0 copy-done
  104.6 3.4 %fusion = f32[8,64,1024]{2,1,0:T(8,128)} fusion(bf16[8,64,768]{2,1,0:T(8,128)(2,1)} %shard_map.64, bf16[768,1024]{1,0:T(8,128)(2,1)S(1)} %copy-done), kind=kOutput, calls=%fused_computation | convolution fusion | flops 805306368 | bytes 4456448 | tf_op jit(solution)/shard_map/sbd,dw->sbw/dot_general | solution.py:445
Async XLA Ops:
  0.0 104.6 %copy-start = (bf16[768,1024]{1,0:T(8,128)(2,1)S(1)}, bf16[768,1024]{1,0:T(8,128)(2,1)}, u32[]{:S(2)}) copy-start(bf16[768,1024]{1,0:T(8,128)(2,1)} %param.11) | copy-start | bytes 4718596

commit v4 on v3

--- a/solution.py
+++ b/solution.py
@@ -90,12 +90,11 @@
         for node in (me, up, down):
             pl.semaphore_signal(barrier, inc=1, device_id=(node, peer), device_id_type=MESH)
     pl.semaphore_wait(barrier, n - 1 + 9)
-    load.wait()
-
-    def ring_copy(slot, m):
+
+    def ring_copy(slot, m, source=None):
         where = pl.ds(pl.multiple_of(side * half + m * piece, piece), piece)
         return pltpu.make_async_remote_copy(
-            src_ref=hold.at[slot, where],
+            src_ref=hold.at[slot, where] if source is None else source.at[0, where],
             dst_ref=hold.at[slot + 1, where],
             send_sem=ring_send.at[slot, m],
             recv_sem=ring_recv.at[slot, m],
@@ -183,7 +182,7 @@
             lax.fori_loop(0, 2, two, 0)
 
     for m in range(PIECES):
-        ring_copy(0, m).start()
+        ring_copy(0, m, factors_ref).start()
 
     def clear(p, _):
         at = pl.ds(pl.multiple_of(p * 4 * rows, 4 * rows), 4 * rows)
@@ -191,13 +190,14 @@
         return 0
 
     lax.fori_loop(0, n, clear, 0)
-
-    levels = vir_table_ref.shape[1]
+    load.wait()
+
+    levels = vir_table_ref.shape[0]
     same = lax.broadcasted_iota(jnp.int32, (levels, levels), 0) == lax.broadcasted_iota(
         jnp.int32, (levels, levels), 1
     )
-    table = jnp.sum(jnp.where(same, vir_table_ref[...], 0.0), axis=1, keepdims=True)
-    hits = lax.broadcasted_iota(jnp.int32, (levels, virt), 0) == vir_level_ref[...]
+    table = jnp.sum(jnp.where(same, vir_table_ref[...].reshape(1, levels), 0.0), axis=1, keepdims=True)
+    hits = lax.broadcasted_iota(jnp.int32, (levels, virt), 0) == vir_level_ref[...].reshape(1, virt)
     row = jnp.sum(jnp.where(hits, table, 0.0), axis=0, keepdims=True)
     ev_row_ref[...] = row
     same = lax.broadcasted_iota(jnp.int32, (virt, virt), 0) == lax.broadcasted_iota(
@@ -302,7 +302,7 @@
 
     @pl.when(late)
     def _():
-        for part in range(2):
+        for part in (side, 1 - side):
             for m in range(PIECES):
                 last_copy(m, part).wait_recv()
             integrals(hops, part)
@@ -328,8 +328,6 @@
             core_copy(k, side, 1).start()
         return 0
 
-    lax.fori_loop(0, n // 2, to_core_late, 0)
-
     def to_owner(t, _):
         k = target(t)
         cross_copy(k).wait_recv()
@@ -348,7 +346,13 @@
 
         return 0
 
-    lax.fori_loop(0, n, to_owner, 0)
+    def finish(t, _):
+        to_core_late(t, 0)
+        for u in range(2):
+            to_owner(2 * t + u, 0)
+        return 0
+
+    lax.fori_loop(0, n // 2, finish, 0)
 
     def settle(t, _):
         k = target(t)
@@ -360,7 +364,7 @@
 
     for slot in range(hops - 1):
         for m in range(PIECES):
-            ring_copy(slot, m).wait_send()
+            ring_copy(slot, m, factors_ref if slot == 0 else None).wait_send()
 
     def sent(slot, _):
         @pl.when(jnp.logical_not(handled(slot)))
@@ -441,7 +445,7 @@
         cost_estimate=pl.CostEstimate(
             flops=8 * virt * virt * naux, bytes_accessed=2 * virt * naux, transcendentals=0
         ),
-    )(occ_level, occupied_energy_levels, factors, vir_level[None, :], vir_table[None, :])
+    )(occ_level, occupied_energy_levels, factors, vir_level, vir_table)
     return jnp.einsum(
         "sbd,dw->sbw",
         gamma_low,

time: 108 us -> 107 us (level)
  local copies, waits for them, and re-layouts: 1.39 us -> 0.01 us
    broadcast_in_dim x1 -> x0, local copies, waits for them, and re-layouts: 1.39 us -> none  [ring_body(): vir_level[None, :]]
where the time goes in v4:
time: 107 us
  Pallas kernels  103 us (96%)
  matrix products  3.44 us (3%)
    pallas_call x1, Pallas kernels, ring_body(): pl.pallas_call(functools.partial(pair_kernel, n), out_shape=jax.ShapeDtyp...  103 us
    dot_general x1, matrix products, ring_body(): jnp.einsum('sbd,dw->sbw', gamma_low, virtual_coefficient_matrix, preferre...  3.44 us

profile of v4, /device:TPU:0, one launch (start us, length us, event | category | flops | bytes accessed | tf_op | source)
XLA Modules:
  0.0 106.9 jit_solution(13108440199895339719)
XLA Ops:
  0.0 0.0 copy-start
  0.0 103.5 %shard_map.64 = bf16[8,64,768]{2,1,0:T(8,128)(2,1)} custom-call(s32[8]{0:T(128)} %occ_level_ref.1, f32[256]{0:T(256)} %occ_table_ref.1, bf16[1,768,2048]{2,1,0:T(8,128)(2,1)} %factors_ref.1, s32[768]{0:T(1024)} %vir_level_ref.1, f32[256]{0:T(256)} %vir_table_ref.1), custom_call_target="tpu_custom_call" | custom-call | flops 9663676416 | bytes 3145728 | tf_op jit(solution)/shard_map/pallas_call | solution.py:406
  103.5 0.0 copy-done
  103.5 3.4 %fusion = f32[8,64,1024]{2,1,0:T(8,128)} fusion(bf16[8,64,768]{2,1,0:T(8,128)(2,1)} %shard_map.64, bf16[768,1024]{1,0:T(8,128)(2,1)S(1)} %copy-done), kind=kOutput, calls=%fused_computation | convolution fusion | flops 805306368 | bytes 4456448 | tf_op jit(solution)/shard_map/sbd,dw->sbw/dot_general | solution.py:449
Async XLA Ops:
  0.0 103.5 %copy-start = (bf16[768,1024]{1,0:T(8,128)(2,1)S(1)}, bf16[768,1024]{1,0:T(8,128)(2,1)}, u32[]{:S(2)}) copy-start(bf16[768,1024]{1,0:T(8,128)(2,1)} %param.11) | copy-start | bytes 4718596
